TPU v7x, 256 devices: a whole 4x4x8 slice. The times are simulated.
256 devices in a mesh: prow: 16 (over z, core), pcol: 16 (over x, y).
Axes of the slice: x: 4, y: 4, z: 8, core: 2. Of those that a mesh axis runs over, the one named last changes fastest.
Arguments:
- leaf_source: bfloat16 [16, 16, 8, 256, 128], P('prow', 'pcol'), may hold values from -6 to 6
- band_source: bfloat16 [16, 256, 128], P('prow'), may hold values from -6 to 6
- strip_source: bfloat16 [16, 256, 128], P('pcol'), may hold values from -6 to 6
- summit_source: bfloat16 [256, 128], replicated, may hold values from -6 to 6
- leaf_inverse: bfloat16 [16, 16, 8, 256, 256], P('prow', 'pcol'), may hold values from -1 to 2
- band_inverse: bfloat16 [16, 256, 256], P('prow'), may hold values from -1 to 2
- strip_inverse: bfloat16 [16, 256, 256], P('pcol'), may hold values from -1 to 2
- summit_inverse: bfloat16 [256, 256], replicated, may hold values from -1 to 2
- leaf_blocks: bfloat16 [16, 16, 28, 256, 256], P('prow', 'pcol'), may hold values from -0.09375 to 0.09375
- band_blocks: bfloat16 [16, 16, 8, 256, 256], P('prow', 'pcol'), may hold values from -0.0234375 to 0.0234375
- strip_blocks: bfloat16 [16, 16, 8, 256, 256], P('prow', 'pcol'), may hold values from -0.0234375 to 0.0234375
- summit_blocks: bfloat16 [16, 16, 8, 256, 256], P('prow', 'pcol'), may hold values from -0.015625 to 0.015625
- coupling: bfloat16 [16, 16, 256, 256], P('prow', 'pcol'), may hold values from -0.0625 to 0.0625
- summit_band: bfloat16 [16, 256, 256], P('prow', 'pcol'), may hold values from -0.046875 to 0.046875
- summit_strip: bfloat16 [16, 256, 256], P('pcol'), may hold values from -0.046875 to 0.046875
- parents: int32 [16, 16, 8], P('prow', 'pcol'), may hold values from 1 to 8, as said below
- widths: int32 [16, 16, 8], P('prow', 'pcol'), may hold values from 64 to 256
Outputs:
- leaf_answer: bfloat16 [16, 16, 8, 256, 128], P('prow', 'pcol')
- band_answer: bfloat16 [16, 256, 128], P('prow')
- strip_answer: bfloat16 [16, 256, 128], P('pcol')
- summit_answer: bfloat16 [256, 128], replicated
Inputs may be any that keep to these rules, and one draw needn't show every extreme that they name: parents[r, c, a] is a later leaf of the same subtree, or 8 where leaf a links only to the separators.
All inputs are finite; a program needn't handle non-finite values.
Results may differ from a plain program's by a relative error of at most 0.015.
Values sent between devices are 32-bit elements; how exact they have to be, the bound alone decides.
A program may use at most 64 MiB of HBM per device.

v0:
```python
import jax
import jax.numpy as jnp
from jax import lax
from jax.sharding import PartitionSpec as P

PASSES = 2


def ancestors(parent_list, leaf_count):
    node_ids = jnp.arange(leaf_count + 1, dtype=jnp.int32)
    current = parent_list
    extended = jnp.concatenate([current, jnp.full((1,), leaf_count, jnp.int32)])
    reached = jnp.zeros((leaf_count + 1, leaf_count), jnp.float32)
    for repeat in range(leaf_count):
        matches = current[None, :] == node_ids[:, None]
        reached = jnp.maximum(reached, matches.astype(jnp.float32))
        current = jnp.sum(jnp.where(matches, extended[:, None], 0), axis=0)
    return reached[:leaf_count]


def multiply(left, right, form):
    return jnp.einsum(form, left, right, preferred_element_type=jnp.float32)


def forward_block(inverse, source, partial_value):
    residual = (source.astype(jnp.float32) - partial_value).astype(jnp.bfloat16)
    return multiply(inverse, residual, "ij,jr->ir").astype(jnp.bfloat16)


def backward_block(inverse, source, partial_value):
    residual = (source.astype(jnp.float32) - partial_value).astype(jnp.bfloat16)
    return multiply(inverse, residual, "ji,jr->ir").astype(jnp.bfloat16)


def leaf_forward(pair_blocks, inverses, sources, reached, row_mask):
    leaf_count = sources.shape[0]
    solved = []
    for position in range(leaf_count):
        residual = sources[position].astype(jnp.float32)
        if position > 0:
            first_pair = position * (position - 1) // 2
            weights = reached[position, :position].astype(jnp.bfloat16)
            stacked = jnp.stack(solved) * weights[:, None, None]
            residual = residual - multiply(
                pair_blocks[first_pair : first_pair + position], stacked, "bij,bjr->ir"
            )
        residual = (row_mask[position] * residual).astype(jnp.bfloat16)
        solved.append(
            (row_mask[position] * multiply(inverses[position], residual, "ij,jr->ir")).astype(
                jnp.bfloat16
            )
        )
    return jnp.stack(solved)


def leaf_backward(pair_blocks, inverses, solved, outer, reached, row_mask):
    leaf_count = solved.shape[0]
    pending = outer
    answers = [None] * leaf_count
    for position in reversed(range(leaf_count)):
        residual = (
            row_mask[position] * (solved[position].astype(jnp.float32) - pending[position])
        ).astype(jnp.bfloat16)
        update = (row_mask[position] * multiply(inverses[position], residual, "ji,jr->ir")).astype(
            jnp.bfloat16
        )
        answers[position] = update
        if position > 0:
            first_pair = position * (position - 1) // 2
            pushed = multiply(
                pair_blocks[first_pair : first_pair + position], update, "bji,jr->bir"
            )
            pending = pending.at[:position].add(
                reached[position, :position][:, None, None] * pushed
            )
    return jnp.stack(answers)


def per_device(
    leaf_source,
    band_source,
    strip_source,
    summit_source,
    leaf_inverse,
    band_inverse,
    strip_inverse,
    summit_inverse,
    leaf_blocks,
    band_blocks,
    strip_blocks,
    summit_blocks,
    coupling,
    summit_band,
    summit_strip,
    parents,
    widths,
):
    leaf_count = leaf_source.shape[2]
    block_width = leaf_source.shape[3]
    reached = ancestors(parents[0, 0], leaf_count)
    column_ids = jnp.arange(block_width, dtype=jnp.int32)
    row_mask = (column_ids[None, :] < widths[0, 0][:, None]).astype(jnp.float32)[:, :, None]
    band_slab = summit_band.shape[1]
    strip_slab = block_width // lax.axis_size("prow")
    column_place = lax.axis_index("pcol") * band_slab
    row_place = lax.axis_index("prow") * strip_slab
    inverses = leaf_inverse[0, 0]
    pair_blocks = leaf_blocks[0, 0]
    to_band = band_blocks[0, 0]
    to_strip = strip_blocks[0, 0]
    to_summit = summit_blocks[0, 0]
    link_block = coupling[0, 0]
    lift_band = summit_band[0]
    lift_strip = summit_strip[0]
    current = (leaf_source[0, 0], band_source[0], strip_source[0], summit_source)
    for iteration in range(PASSES):
        leaf_now, band_now, strip_now, summit_now = current
        solved = leaf_forward(pair_blocks, inverses, leaf_now, reached, row_mask)
        band_term = multiply(to_band, solved, "aij,ajr->ir")
        strip_term = multiply(to_strip, solved, "aij,ajr->ir")
        summit_term = multiply(to_summit, solved, "aij,ajr->ir")
        band_partial = lax.psum(band_term, "pcol")
        band_solved = forward_block(band_inverse[0], band_now, band_partial)
        own_band = lax.dynamic_slice_in_dim(band_solved, column_place, band_slab, 0)
        summit_term = summit_term + multiply(lift_band, own_band, "ki,kn->in")
        strip_term = strip_term + multiply(link_block, band_solved, "ij,jn->in")
        strip_partial = lax.psum(strip_term, "prow")
        strip_solved = forward_block(strip_inverse[0], strip_now, strip_partial)
        own_lift = lax.dynamic_slice_in_dim(lift_strip, row_place, strip_slab, 0)
        own_strip = lax.dynamic_slice_in_dim(strip_solved, row_place, strip_slab, 0)
        summit_partial = lax.psum(
            summit_term + multiply(own_lift, own_strip, "ki,kn->in"), ("prow", "pcol")
        )
        summit_solved = forward_block(summit_inverse, summit_now, summit_partial)
        summit_answer = backward_block(
            summit_inverse, summit_solved, jnp.zeros(summit_solved.shape, jnp.float32)
        )
        strip_answer = backward_block(
            strip_inverse[0], strip_solved, multiply(lift_strip, summit_answer, "ki,in->kn")
        )
        downward = multiply(link_block, strip_answer, "ji,jn->in")
        band_piece = multiply(lift_band, summit_answer, "ki,in->kn")
        band_back = lax.psum(downward, "pcol") + lax.all_gather(
            band_piece, "pcol", axis=0, tiled=True
        )
        band_answer = backward_block(band_inverse[0], band_solved, band_back)
        outer = (
            multiply(to_band, band_answer, "aij,ir->ajr")
            + multiply(to_strip, strip_answer, "aij,ir->ajr")
            + multiply(to_summit, summit_answer, "aij,ir->ajr")
        )
        leaf_answer = leaf_backward(pair_blocks, inverses, solved, outer, reached, row_mask)
        current = (leaf_answer, band_answer, strip_answer, summit_answer)
    return (current[0][None, None], current[1][None], current[2][None], current[3])


def solution(mesh):
    placed = (
        P("prow", "pcol", None, None, None),
        P("prow", None, None),
        P("pcol", None, None),
        P(),
        P("prow", "pcol", None, None, None),
        P("prow", None, None),
        P("pcol", None, None),
        P(),
        P("prow", "pcol", None, None, None),
        P("prow", "pcol", None, None, None),
        P("prow", "pcol", None, None, None),
        P("prow", "pcol", None, None, None),
        P("prow", "pcol", None, None),
        P("prow", "pcol", None),
        P("pcol", None, None),
        P("prow", "pcol", None),
        P("prow", "pcol", None),
    )
    return jax.shard_map(
        per_device,
        mesh=mesh,
        in_specs=placed,
        out_specs=(
            P("prow", "pcol", None, None, None),
            P("prow", None, None),
            P("pcol", None, None),
            P(),
        ),
        check_vma=False,
    )
```

profile of v0, /device:TPU:2, one launch (start us, length us, event | category | flops | bytes accessed | tf_op | source)
XLA Modules:
  0.0 1181.8 jit_solution(3843605746356094015)
XLA Ops:
  22.1 2.2 constant_dynamic-update-slice_fusion.13
  25.3 2.5 constant_dynamic-update-slice_fusion.12
  28.6 2.6 constant_dynamic-update-slice_fusion.11
  31.2 2.6 constant_dynamic-update-slice_fusion.18
  33.8 2.2 convolution_bitcast_fusion.19
  46.5 84.6 %all-reduce.9.cloned.1.call-done = f32[256,128]{1,0:T(8,128)} async-done(((f32[256,128]{1,0:T(8,128)}), f32[256,128]{1,0:T(8,128)}) %all-reduce.9.cloned.1.call-update) | async-done | bytes 131088 | tf_op jit(solution)/shard_map/psum | solution.py:122
  136.7 105.3 %all-reduce.11.cloned.1.call-done = f32[256,128]{1,0:T(8,128)} async-done(((f32[256,128]{1,0:T(8,128)}), f32[256,128]{1,0:T(8,128)}) %all-reduce.11.cloned.1.call-update) | async-done | bytes 131088 | tf_op jit(solution)/shard_map/psum | solution.py:127
  246.8 243.6 %all-reduce.13.cloned.1.call-done = f32[256,128]{1,0:T(8,128)} async-done(((f32[256,128]{1,0:T(8,128)}), f32[256,128]{1,0:T(8,128)}) %all-reduce.13.cloned.1.call-update) | async-done | bytes 131088 | tf_op jit(solution)/shard_map/psum | solution.py:131
  496.9 23.8 %all_gather.6 = f32[256,128]{1,0:T(8,128)} all-gather(f32[16,128]{1,0:T(8,128)S(1)} %convolution_bitcast_fusion.22), channel_id=1, replica_groups=mesh['prow'=16,'pcol'=16] {'pcol'}, dimensions={0}, use_global_device_ids=true | all-gather | bytes 139264 | tf_op jit(solution)/shard_map/all_gather | solution.py:143
  522.3 62.3 %all-reduce.15.cloned.1.call-done = f32[256,128]{0,1:T(8,128)} async-done(((f32[256,128]{0,1:T(8,128)}), f32[256,128]{0,1:T(8,128)}) %all-reduce.15.cloned.1.call-update) | async-done | bytes 131088 | tf_op jit(solution)/shard_map/psum | solution.py:143
  599.0 2.2 constant_dynamic-update-slice_fusion.41
  601.2 2.4 constant_dynamic-update-slice_fusion.40
  603.6 2.4 constant_dynamic-update-slice_fusion.39
  606.0 2.5 constant_dynamic-update-slice_fusion.38
  608.5 2.6 constant_dynamic-update-slice_fusion.37
  611.1 2.7 constant_dynamic-update-slice_fusion.44
  613.8 2.2 convolution_bitcast_fusion.13
  616.0 2.2 convolution_bitcast_fusion.15
  618.2 2.2 convolution_bitcast_fusion.14
  620.4 89.7 %all-reduce.17.cloned.1.call-done = f32[256,128]{0,1:T(8,128)} async-done(((f32[256,128]{0,1:T(8,128)}), f32[256,128]{0,1:T(8,128)}) %all-reduce.17.cloned.1.call-update) | async-done | bytes 131088 | tf_op jit(solution)/shard_map/psum | solution.py:122
  715.6 105.4 %all-reduce.19.cloned.1.call-done = f32[256,128]{0,1:T(8,128)} async-done(((f32[256,128]{0,1:T(8,128)}), f32[256,128]{0,1:T(8,128)}) %all-reduce.19.cloned.1.call-update) | async-done | bytes 131088 | tf_op jit(solution)/shard_map/psum | solution.py:127
  824.6 245.8 %all-reduce.21.cloned.1.call-done = f32[256,128]{0,1:T(8,128)} async-done(((f32[256,128]{0,1:T(8,128)}), f32[256,128]{0,1:T(8,128)}) %all-reduce.21.cloned.1.call-update) | async-done | bytes 131088 | tf_op jit(solution)/shard_map/psum | solution.py:131
  1077.7 22.2 %all_gather.7 = f32[256,128]{1,0:T(8,128)S(1)} all-gather(f32[16,128]{1,0:T(8,128)S(1)} %convolution_bitcast_fusion.21), channel_id=1, replica_groups=mesh['prow'=16,'pcol'=16] {'pcol'}, dimensions={0}, use_global_device_ids=true | all-gather | bytes 139264 | tf_op jit(solution)/shard_map/all_gather | solution.py:143
  1100.7 62.5 %all-reduce.23.cloned.1.call-done = f32[256,128]{0,1:T(8,128)} async-done(((f32[256,128]{0,1:T(8,128)}), f32[256,128]{0,1:T(8,128)}) %all-reduce.23.cloned.1.call-update) | async-done | bytes 131088 | tf_op jit(solution)/shard_map/psum | solution.py:143
  (293 shorter events, 86.9 us)
Async XLA Ops:
  7.2 26.6 %copy-start = (bf16[1,1,8,256,256]{4,3,2,1,0:T(8,128)(2,1)S(1)}, bf16[1,1,8,256,256]{4,3,2,1,0:T(8,128)(2,1)}, u32[]{:S(2)}) copy-start(bf16[1,1,8,256,256]{4,3,2,1,0:T(8,128)(2,1)} %param.54) | copy-start | bytes 3145732
  7.2 124.0 %all-reduce.9.cloned.1.call-start = ((), (), s32[]{:S(2)}) async-start(), calls=%async_computation | async-start | bytes 262144 | tf_op jit(solution)/shard_map/psum | solution.py:122
  10.6 20.6 %copy-start.79 = (bf16[7]{0:T(256)(128)(2,1)}, bf16[7]{0:T(256)(128)(2,1)S(1)}, u32[]{:S(2)}) copy-start(bf16[7]{0:T(256)(128)(2,1)S(1)} %fusion.590) | copy-start | bytes 46
  10.6 18.0 %copy-start.80 = (bf16[6]{0:T(256)(128)(2,1)}, bf16[6]{0:T(256)(128)(2,1)S(1)}, u32[]{:S(2)}) copy-start(bf16[6]{0:T(256)(128)(2,1)S(1)} %fusion.589) | copy-start | bytes 40
  10.6 14.7 %copy-start.81 = (bf16[5]{0:T(256)(128)(2,1)}, bf16[5]{0:T(256)(128)(2,1)S(1)}, u32[]{:S(2)}) copy-start(bf16[5]{0:T(256)(128)(2,1)S(1)} %fusion.588) | copy-start | bytes 34
  10.7 13.6 %copy-start.82 = (bf16[4]{0:T(256)(128)(2,1)}, bf16[4]{0:T(256)(128)(2,1)S(1)}, u32[]{:S(2)}) copy-start(bf16[4]{0:T(256)(128)(2,1)S(1)} %fusion.587) | copy-start | bytes 28
  10.7 13.6 %copy-start.83 = (bf16[3]{0:T(256)(128)(2,1)}, bf16[3]{0:T(256)(128)(2,1)S(1)}, u32[]{:S(2)}) copy-start(bf16[3]{0:T(256)(128)(2,1)S(1)} %fusion.586) | copy-start | bytes 22
  10.7 13.6 %copy-start.84 = (bf16[2]{0:T(256)(128)(2,1)}, bf16[2]{0:T(256)(128)(2,1)S(1)}, u32[]{:S(2)}) copy-start(bf16[2]{0:T(256)(128)(2,1)S(1)} %fusion.585) | copy-start | bytes 16
  12.2 16.4 %copy-start.54 = (f32[1,256]{1,0:T(1,128)}, f32[1,256]{1,0:T(1,128)S(1)}, u32[]{:S(2)}) copy-start(f32[1,256]{1,0:T(1,128)S(1)} %get-tuple-element.238) | copy-start | bytes 3076
  12.2 19.0 %copy-start.57 = (f32[1,256]{1,0:T(1,128)}, f32[1,256]{1,0:T(1,128)S(1)}, u32[]{:S(2)}) copy-start(f32[1,256]{1,0:T(1,128)S(1)} %get-tuple-element.237) | copy-start | bytes 3076
  25.3 17.0 %copy-start.2 = (bf16[1,1,8,256,256]{4,3,2,1,0:T(8,128)(2,1)S(1)}, bf16[1,1,8,256,256]{4,3,2,1,0:T(8,128)(2,1)}, u32[]{:S(2)}) copy-start(bf16[1,1,8,256,256]{4,3,2,1,0:T(8,128)(2,1)} %param.56) | copy-start | bytes 3145732
  28.6 15.8 %copy-start.1 = (bf16[1,1,8,256,256]{4,3,2,1,0:T(8,128)(2,1)S(1)}, bf16[1,1,8,256,256]{4,3,2,1,0:T(8,128)(2,1)}, u32[]{:S(2)}) copy-start(bf16[1,1,8,256,256]{4,3,2,1,0:T(8,128)(2,1)} %param.55) | copy-start | bytes 3145732
  31.2 101.8 %copy-start.9 = (bf16[1,1,256,256]{3,2,1,0:T(8,128)(2,1)S(1)}, bf16[1,1,256,256]{3,2,1,0:T(8,128)(2,1)}, u32[]{:S(2)}) copy-start(bf16[1,1,256,256]{3,2,1,0:T(8,128)(2,1)} %param.57) | copy-start | bytes 393220
  33.8 101.0 %copy-start.25 = (bf16[1,16,256]{2,1,0:T(8,128)(2,1)S(1)}, bf16[1,16,256]{2,1,0:T(8,128)(2,1)}, u32[]{:S(2)}) copy-start(bf16[1,16,256]{2,1,0:T(8,128)(2,1)} %param.58) | copy-start | bytes 24580
  33.8 208.2 %copy-start.8 = (bf16[1,256,256]{2,1,0:T(8,128)(2,1)S(1)}, bf16[1,256,256]{2,1,0:T(8,128)(2,1)}, u32[]{:S(2)}) copy-start(bf16[1,256,256]{2,1,0:T(8,128)(2,1)} %param.51) | copy-start | bytes 393220
  33.8 456.7 %copy-start.10 = (bf16[256,256]{1,0:T(8,128)(2,1)S(1)}, bf16[256,256]{1,0:T(8,128)(2,1)}, u32[]{:S(2)}) copy-start(bf16[256,256]{1,0:T(8,128)(2,1)} %param.52) | copy-start | bytes 393220
  36.0 206.0 %all-reduce.11.cloned.1.call-start = ((), (), s32[]{:S(2)}) async-start(), calls=%async_computation.1 | async-start | bytes 262144 | tf_op jit(solution)/shard_map/psum | solution.py:127
  134.8 355.7 %all-reduce.13.cloned.1.call-start = ((), (), s32[]{:S(2)}) async-start(), calls=%async_computation.2 | async-start | bytes 262144 | tf_op jit(solution)/shard_map/psum | solution.py:131
  245.6 339.0 %all-reduce.15.cloned.1.call-start = ((), (), s32[]{:S(2)}) async-start(), calls=%async_computation.3 | async-start | bytes 262144 | tf_op jit(solution)/shard_map/psum | solution.py:143
  495.9 214.2 %all-reduce.17.cloned.1.call-start = ((), (), s32[]{:S(2)}) async-start(), calls=%async_computation.4 | async-start | bytes 262144 | tf_op jit(solution)/shard_map/psum | solution.py:122
  618.2 202.9 %all-reduce.19.cloned.1.call-start = ((), (), s32[]{:S(2)}) async-start(), calls=%async_computation.5 | async-start | bytes 262144 | tf_op jit(solution)/shard_map/psum | solution.py:127
  713.8 356.7 %all-reduce.21.cloned.1.call-start = ((), (), s32[]{:S(2)}) async-start(), calls=%async_computation.6 | async-start | bytes 262144 | tf_op jit(solution)/shard_map/psum | solution.py:131
  824.6 338.6 %all-reduce.23.cloned.1.call-start = ((), (), s32[]{:S(2)}) async-start(), calls=%async_computation.7 | async-start | bytes 262144 | tf_op jit(solution)/shard_map/psum | solution.py:143
  1073.5 94.6 %copy-start.11 = (bf16[128,256]{1,0:T(8,128)(2,1)S(1)}, bf16[128,256]{1,0:T(8,128)(2,1)}, u32[]{:S(2)}) copy-start(bf16[128,256]{1,0:T(8,128)(2,1)} %convolution_convert_fusion.2) | copy-start | bytes 196612
  (69 other events, 185.5 us)
Sparse Core Ops, SparseCore 0:
  36.1 94.9 all-reduce.8
  134.9 107.0 all-reduce.10
  248.1 242.3 all-reduce.12
  496.0 88.5 all-reduce.14
  618.3 91.8 all-reduce.16
  713.9 107.1 all-reduce.18
  828.0 242.3 all-reduce.20
  1074.5 88.5 all-reduce.22
where the time goes:
time: 1180 us
  waiting for transfers between devices  999 us (85%)
  matrix products  92.7 us (8%)
  blocking collectives  46 us (4%)
  local copies, waits for them, and re-layouts  23.6 us (2%)
  between operations  16.2 us (1%)
    psum x2, waiting for transfers between devices, per_device(): lax.psum(summit_term + multiply(own_lift, own_strip, 'ki,kn->in'), ('prow...  489 us
    psum x2, waiting for transfers between devices, per_device(): strip_partial = lax.psum(strip_term, 'prow')  211 us
    psum x2, waiting for transfers between devices, per_device(): band_partial = lax.psum(band_term, 'pcol')  174 us
    psum x2, waiting for transfers between devices, per_device(): lax.psum(downward, 'pcol')  125 us
    dot_general x76, matrix products, multiply(): return jnp.einsum(form, left, right, preferred_element_type=jnp.float32)  92.7 us
    all_gather x2, blocking collectives, per_device(): lax.all_gather(band_piece, 'pcol', axis=0, tiled=True)  46 us
  transfers between devices with their start and end apart: 8, of which 8 were waited for; matrix products, arithmetic and copies ran while one was open for 2% of the time, Pallas kernels for 0%

commit v1 on v0

--- a/solution.py
+++ b/solution.py
@@ -128,9 +128,8 @@
         strip_solved = forward_block(strip_inverse[0], strip_now, strip_partial)
         own_lift = lax.dynamic_slice_in_dim(lift_strip, row_place, strip_slab, 0)
         own_strip = lax.dynamic_slice_in_dim(strip_solved, row_place, strip_slab, 0)
-        summit_partial = lax.psum(
-            summit_term + multiply(own_lift, own_strip, "ki,kn->in"), ("prow", "pcol")
-        )
+        t0 = summit_term + multiply(own_lift, own_strip, "ki,kn->in")
+        summit_partial = jax.lax.psum(jax.lax.psum(t0, "pcol"), "prow")
         summit_solved = forward_block(summit_inverse, summit_now, summit_partial)
         summit_answer = backward_block(
             summit_inverse, summit_solved, jnp.zeros(summit_solved.shape, jnp.float32)

time: 1180 us -> 1110 us (0.941)
  waiting for transfers between devices: 999 us -> 918 us
    psum x2 -> x4, waiting for transfers between devices: 489 us -> 402 us  [per_device(): summit_partial = jax.lax.psum(jax.lax.psum(t0, 'pcol'), 'prow')]
  transfers between devices with their start and end apart: 8 -> 10, of which waited for: 8 -> 10; matrix products, arithmetic and copies ran while one was open for 2% -> 2% of each run, Pallas kernels for 0% -> 0%
where the time goes in v1:
time: 1110 us; the launch traced here: 1100 us
  waiting for transfers between devices  918 us (83%)
  matrix products  92.7 us (8%)
  blocking collectives  48.6 us (4%)
  local copies, waits for them, and re-layouts  23.6 us (2%)
  between operations  16.2 us (1%)
    psum x4, waiting for transfers between devices, per_device(): summit_partial = jax.lax.psum(jax.lax.psum(t0, 'pcol'), 'prow')  402 us
    psum x2, waiting for transfers between devices, per_device(): strip_partial = lax.psum(strip_term, 'prow')  211 us
    psum x2, waiting for transfers between devices, per_device(): band_partial = lax.psum(band_term, 'pcol')  176 us
    psum x2, waiting for transfers between devices, per_device(): lax.psum(downward, 'pcol')  130 us
    dot_general x76, matrix products, multiply(): return jnp.einsum(form, left, right, preferred_element_type=jnp.float32)  92.7 us
    all_gather x2, blocking collectives, per_device(): lax.all_gather(band_piece, 'pcol', axis=0, tiled=True)  48.6 us
  transfers between devices with their start and end apart: 10, of which 10 were waited for; matrix products, arithmetic and copies ran while one was open for 2% of the time, Pallas kernels for 0%

profile of v1, /device:TPU:2, one launch (start us, length us, event | category | flops | bytes accessed | tf_op | source)
XLA Modules:
  0.0 1103.5 jit_solution(17837924078660387973)
XLA Ops:
  22.1 2.2 constant_dynamic-update-slice_fusion.13
  25.3 2.5 constant_dynamic-update-slice_fusion.12
  28.6 2.6 constant_dynamic-update-slice_fusion.11
  31.2 2.6 constant_dynamic-update-slice_fusion.18
  45.3 85.9 %all-reduce.11.cloned.1.call-done = f32[256,128]{1,0:T(8,128)} async-done(((f32[256,128]{1,0:T(8,128)}), f32[256,128]{1,0:T(8,128)}) %all-reduce.11.cloned.1.call-update) | async-done | bytes 131088 | tf_op jit(solution)/shard_map/psum | solution.py:122
  136.7 105.4 %all-reduce.13.cloned.1.call-done = f32[256,128]{1,0:T(8,128)} async-done(((f32[256,128]{1,0:T(8,128)}), f32[256,128]{1,0:T(8,128)}) %all-reduce.13.cloned.1.call-update) | async-done | bytes 131088 | tf_op jit(solution)/shard_map/psum | solution.py:127
  246.8 91.5 %all-reduce.15.cloned.1.call-done = f32[256,128]{1,0:T(8,128)} async-done(((f32[256,128]{1,0:T(8,128)}), f32[256,128]{1,0:T(8,128)}) %all-reduce.15.cloned.1.call-update) | async-done | bytes 131088 | tf_op jit(solution)/shard_map/psum | solution.py:132
  339.6 108.2 %all-reduce.17.cloned.1.call-done = f32[256,128]{1,0:T(8,128)} async-done(((f32[256,128]{1,0:T(8,128)}), f32[256,128]{1,0:T(8,128)}) %all-reduce.17.cloned.1.call-update) | async-done | bytes 131088 | tf_op jit(solution)/shard_map/psum | solution.py:132
  454.2 25.1 %all_gather.6 = f32[256,128]{1,0:T(8,128)} all-gather(f32[16,128]{1,0:T(8,128)S(1)} %convolution_bitcast_fusion.22), channel_id=1, replica_groups=mesh['prow'=16,'pcol'=16] {'pcol'}, dimensions={0}, use_global_device_ids=true | all-gather | bytes 139264 | tf_op jit(solution)/shard_map/all_gather | solution.py:142
  481.0 64.8 %all-reduce.19.cloned.1.call-done = f32[256,128]{0,1:T(8,128)} async-done(((f32[256,128]{0,1:T(8,128)}), f32[256,128]{0,1:T(8,128)}) %all-reduce.19.cloned.1.call-update) | async-done | bytes 131088 | tf_op jit(solution)/shard_map/psum | solution.py:142
  560.2 2.2 constant_dynamic-update-slice_fusion.41
  562.4 2.4 constant_dynamic-update-slice_fusion.40
  564.8 2.4 constant_dynamic-update-slice_fusion.39
  567.2 2.5 constant_dynamic-update-slice_fusion.38
  569.7 2.6 constant_dynamic-update-slice_fusion.37
  572.3 2.7 constant_dynamic-update-slice_fusion.44
  575.0 2.2 convolution_bitcast_fusion.13
  579.4 2.2 convolution_bitcast_fusion.14
  581.6 89.7 %all-reduce.21.cloned.1.call-done = f32[256,128]{0,1:T(8,128)} async-done(((f32[256,128]{0,1:T(8,128)}), f32[256,128]{0,1:T(8,128)}) %all-reduce.21.cloned.1.call-update) | async-done | bytes 131088 | tf_op jit(solution)/shard_map/psum | solution.py:122
  676.8 105.4 %all-reduce.23.cloned.1.call-done = f32[256,128]{0,1:T(8,128)} async-done(((f32[256,128]{0,1:T(8,128)}), f32[256,128]{0,1:T(8,128)}) %all-reduce.23.cloned.1.call-update) | async-done | bytes 131088 | tf_op jit(solution)/shard_map/psum | solution.py:127
  785.8 93.0 %all-reduce.25.cloned.1.call-done = f32[256,128]{0,1:T(8,128)} async-done(((f32[256,128]{0,1:T(8,128)}), f32[256,128]{0,1:T(8,128)}) %all-reduce.25.cloned.1.call-update) | async-done | bytes 131088 | tf_op jit(solution)/shard_map/psum | solution.py:132
  878.9 109.4 %all-reduce.27.cloned.1.call-done = f32[256,128]{0,1:T(8,128)} async-done(((f32[256,128]{0,1:T(8,128)}), f32[256,128]{0,1:T(8,128)}) %all-reduce.27.cloned.1.call-update) | async-done | bytes 131088 | tf_op jit(solution)/shard_map/psum | solution.py:132
  995.5 23.5 %all_gather.7 = f32[256,128]{1,0:T(8,128)S(1)} all-gather(f32[16,128]{1,0:T(8,128)S(1)} %convolution_bitcast_fusion.21), channel_id=1, replica_groups=mesh['prow'=16,'pcol'=16] {'pcol'}, dimensions={0}, use_global_device_ids=true | all-gather | bytes 139264 | tf_op jit(solution)/shard_map/all_gather | solution.py:142
  1019.8 65.1 %all-reduce.29.cloned.1.call-done = f32[256,128]{0,1:T(8,128)} async-done(((f32[256,128]{0,1:T(8,128)}), f32[256,128]{0,1:T(8,128)}) %all-reduce.29.cloned.1.call-update) | async-done | bytes 131088 | tf_op jit(solution)/shard_map/psum | solution.py:142
  (299 shorter events, 91.3 us)
Async XLA Ops:
  7.2 26.6 %copy-start = (bf16[1,1,8,256,256]{4,3,2,1,0:T(8,128)(2,1)S(1)}, bf16[1,1,8,256,256]{4,3,2,1,0:T(8,128)(2,1)}, u32[]{:S(2)}) copy-start(bf16[1,1,8,256,256]{4,3,2,1,0:T(8,128)(2,1)} %param.54) | copy-start | bytes 3145732
  7.2 124.0 %all-reduce.11.cloned.1.call-start = ((), (), s32[]{:S(2)}) async-start(), calls=%async_computation | async-start | bytes 262144 | tf_op jit(solution)/shard_map/psum | solution.py:122
  10.6 20.6 %copy-start.79 = (bf16[7]{0:T(256)(128)(2,1)}, bf16[7]{0:T(256)(128)(2,1)S(1)}, u32[]{:S(2)}) copy-start(bf16[7]{0:T(256)(128)(2,1)S(1)} %fusion.590) | copy-start | bytes 46
  10.6 18.0 %copy-start.80 = (bf16[6]{0:T(256)(128)(2,1)}, bf16[6]{0:T(256)(128)(2,1)S(1)}, u32[]{:S(2)}) copy-start(bf16[6]{0:T(256)(128)(2,1)S(1)} %fusion.589) | copy-start | bytes 40
  10.6 14.7 %copy-start.81 = (bf16[5]{0:T(256)(128)(2,1)}, bf16[5]{0:T(256)(128)(2,1)S(1)}, u32[]{:S(2)}) copy-start(bf16[5]{0:T(256)(128)(2,1)S(1)} %fusion.588) | copy-start | bytes 34
  10.7 13.6 %copy-start.82 = (bf16[4]{0:T(256)(128)(2,1)}, bf16[4]{0:T(256)(128)(2,1)S(1)}, u32[]{:S(2)}) copy-start(bf16[4]{0:T(256)(128)(2,1)S(1)} %fusion.587) | copy-start | bytes 28
  12.2 16.4 %copy-start.54 = (f32[1,256]{1,0:T(1,128)}, f32[1,256]{1,0:T(1,128)S(1)}, u32[]{:S(2)}) copy-start(f32[1,256]{1,0:T(1,128)S(1)} %get-tuple-element.238) | copy-start | bytes 3076
  12.2 19.0 %copy-start.57 = (f32[1,256]{1,0:T(1,128)}, f32[1,256]{1,0:T(1,128)S(1)}, u32[]{:S(2)}) copy-start(f32[1,256]{1,0:T(1,128)S(1)} %get-tuple-element.237) | copy-start | bytes 3076
  25.3 15.7 %copy-start.2 = (bf16[1,1,8,256,256]{4,3,2,1,0:T(8,128)(2,1)S(1)}, bf16[1,1,8,256,256]{4,3,2,1,0:T(8,128)(2,1)}, u32[]{:S(2)}) copy-start(bf16[1,1,8,256,256]{4,3,2,1,0:T(8,128)(2,1)} %param.56) | copy-start | bytes 3145732
  28.6 14.6 %copy-start.1 = (bf16[1,1,8,256,256]{4,3,2,1,0:T(8,128)(2,1)S(1)}, bf16[1,1,8,256,256]{4,3,2,1,0:T(8,128)(2,1)}, u32[]{:S(2)}) copy-start(bf16[1,1,8,256,256]{4,3,2,1,0:T(8,128)(2,1)} %param.55) | copy-start | bytes 3145732
  31.2 101.8 %copy-start.9 = (bf16[1,1,256,256]{3,2,1,0:T(8,128)(2,1)S(1)}, bf16[1,1,256,256]{3,2,1,0:T(8,128)(2,1)}, u32[]{:S(2)}) copy-start(bf16[1,1,256,256]{3,2,1,0:T(8,128)(2,1)} %param.57) | copy-start | bytes 393220
  33.8 101.0 %copy-start.25 = (bf16[1,16,256]{2,1,0:T(8,128)(2,1)S(1)}, bf16[1,16,256]{2,1,0:T(8,128)(2,1)}, u32[]{:S(2)}) copy-start(bf16[1,16,256]{2,1,0:T(8,128)(2,1)} %param.58) | copy-start | bytes 24580
  33.8 208.2 %copy-start.8 = (bf16[1,256,256]{2,1,0:T(8,128)(2,1)S(1)}, bf16[1,256,256]{2,1,0:T(8,128)(2,1)}, u32[]{:S(2)}) copy-start(bf16[1,256,256]{2,1,0:T(8,128)(2,1)} %param.51) | copy-start | bytes 393220
  33.8 413.9 %copy-start.10 = (bf16[256,256]{1,0:T(8,128)(2,1)S(1)}, bf16[256,256]{1,0:T(8,128)(2,1)}, u32[]{:S(2)}) copy-start(bf16[256,256]{1,0:T(8,128)(2,1)} %param.52) | copy-start | bytes 393220
  36.0 206.0 %all-reduce.13.cloned.1.call-start = ((), (), s32[]{:S(2)}) async-start(), calls=%async_computation.1 | async-start | bytes 262144 | tf_op jit(solution)/shard_map/psum | solution.py:127
  134.8 203.6 %all-reduce.15.cloned.1.call-start = ((), (), s32[]{:S(2)}) async-start(), calls=%async_computation.2 | async-start | bytes 262144 | tf_op jit(solution)/shard_map/psum | solution.py:132
  245.6 202.1 %all-reduce.17.cloned.1.call-start = ((), (), s32[]{:S(2)}) async-start(), calls=%async_computation.3 | async-start | bytes 262144 | tf_op jit(solution)/shard_map/psum | solution.py:132
  338.3 207.5 %all-reduce.19.cloned.1.call-start = ((), (), s32[]{:S(2)}) async-start(), calls=%async_computation.4 | async-start | bytes 262144 | tf_op jit(solution)/shard_map/psum | solution.py:142
  453.1 218.1 %all-reduce.21.cloned.1.call-start = ((), (), s32[]{:S(2)}) async-start(), calls=%async_computation.5 | async-start | bytes 262144 | tf_op jit(solution)/shard_map/psum | solution.py:122
  579.3 202.8 %all-reduce.23.cloned.1.call-start = ((), (), s32[]{:S(2)}) async-start(), calls=%async_computation.6 | async-start | bytes 262144 | tf_op jit(solution)/shard_map/psum | solution.py:127
  674.9 203.9 %all-reduce.25.cloned.1.call-start = ((), (), s32[]{:S(2)}) async-start(), calls=%async_computation.7 | async-start | bytes 262144 | tf_op jit(solution)/shard_map/psum | solution.py:132
  785.7 202.5 %all-reduce.27.cloned.1.call-start = ((), (), s32[]{:S(2)}) async-start(), calls=%async_computation.8 | async-start | bytes 262144 | tf_op jit(solution)/shard_map/psum | solution.py:132
  878.8 206.1 %all-reduce.29.cloned.1.call-start = ((), (), s32[]{:S(2)}) async-start(), calls=%async_computation.9 | async-start | bytes 262144 | tf_op jit(solution)/shard_map/psum | solution.py:142
  991.4 98.5 %copy-start.11 = (bf16[128,256]{1,0:T(8,128)(2,1)S(1)}, bf16[128,256]{1,0:T(8,128)(2,1)}, u32[]{:S(2)}) copy-start(bf16[128,256]{1,0:T(8,128)(2,1)} %convolution_convert_fusion.2) | copy-start | bytes 196612
  (71 other events, 212.7 us)
Sparse Core Ops, SparseCore 0:
  36.1 94.9 all-reduce.10
  134.9 107.0 all-reduce.12
  245.8 92.4 all-reduce.14
  340.6 107.0 all-reduce.16
  453.3 92.4 all-reduce.18
  579.5 91.7 all-reduce.20
  675.0 107.1 all-reduce.22
  786.3 92.4 all-reduce.24
  881.1 107.0 all-reduce.26
  992.3 92.4 all-reduce.28
